TPU v7x, 32 devices: a whole 2x2x4 slice. The times are simulated.
32 devices in a mesh: dp: 4 (over z), mp: 8 (over y, x, core).
Axes of the slice: x: 2, y: 2, z: 4, core: 2. Of those that a mesh axis runs over, the one named last changes fastest.
Arguments:
- guess_vectors: bfloat16 [128, 16, 4096], P(('dp', 'mp')), may hold values from -6 to 6
- preceding_symbol_vector: bfloat16 [128, 4096], P(('dp', 'mp')), may hold values from -6 to 6
- earlier_memory_matrix: float32 [128, 64, 64, 64], P('dp', 'mp'), may hold values from -4 to 4
- lag_blend_factor: float32 [4096], replicated, may hold values from 0 to 1
- constant_lag_blends: float32 [5, 4096], replicated, may hold values from 0 to 1
- blending_lower_matrix: bfloat16 [4096, 160], replicated, may hold values from -0.09375 to 0.09375
- blending_raise_matrix: bfloat16 [5, 32, 4096], replicated, may hold values from -1 to 1
- constant_fading: float32 [4096], P('mp'), may hold values from -6 to -1
- fading_lower_matrix: bfloat16 [4096, 64], replicated, may hold values from -0.09375 to 0.09375
- fading_raise_matrix: bfloat16 [64, 4096], P(None, 'mp'), may hold values from -1 to 1
- diagonal_boost: float32 [64, 64], P('mp'), may hold values from -3 to 3
- acceptor_matrix: bfloat16 [4096, 4096], P('dp', 'mp'), may hold values from -0.09375 to 0.09375
- lookup_matrix: bfloat16 [4096, 4096], P('dp', 'mp'), may hold values from -0.09375 to 0.09375
- payload_matrix: bfloat16 [4096, 4096], P('dp', 'mp'), may hold values from -0.09375 to 0.09375
- gating_matrix: bfloat16 [4096, 4096], P('dp', 'mp'), may hold values from -0.09375 to 0.09375
- emission_matrix: bfloat16 [4096, 4096], P('mp', 'dp'), may hold values from -0.09375 to 0.09375
- groupwise_scaling_factor: float32 [4096], P('mp'), may hold values from 0.1 to 1.9
- groupwise_scaling_offset: float32 [4096], P('mp'), may hold values from -3 to 3
- usable_guess_amount: int32 [128], replicated, may hold values from 1 to 16, as said below
- approved_guesses: int32 [128], replicated, may hold values from 0 to 16, as said below
- destination_slot: int32 [128], replicated, may hold values from 0 to 127, as said below
Outputs:
- layer_out: bfloat16 [128, 16, 4096], P(('dp', 'mp'))
- next_state: float32 [128, 64, 64, 64], P('dp', 'mp')
- next_edge: bfloat16 [128, 4096], P('dp', 'mp')
Inputs may be any that keep to these rules, and one draw needn't show every extreme that they name: `usable_guess_amount`: some request has all 16 draft tokens valid. approved_guesses[b] <= usable_guess_amount[b]; some request accepts all 16. destination_slot is a permutation of the requests. Of the 32 requests of one aligned block, at most 16 have owner slots in one aligned block of 32 slots, and some pair of blocks reaches 16.
All inputs are finite; a program needn't handle non-finite values.
Results may differ from a plain program's by a relative error of at most 0.007.
Values may be sent and summed in bfloat16 or wider, within the bound.
A program may use at most 256 MiB of HBM per device.

v0:
```python
import jax
import jax.numpy as jnp
from jax import lax
from jax.sharding import PartitionSpec as P

GROUP_DIMENSION = 64
norm_eps = 0.00064


def token_mixes(
    guess_vectors,
    edges,
    lag_blend_factor,
    constant_lag_blends,
    blending_lower_matrix,
    blending_raise_matrix,
):
    previous = jnp.concatenate([edges[:, None, :], guess_vectors[:, :-1, :]], axis=1)
    width = guess_vectors.shape[-1]
    current_input = guess_vectors.reshape(-1, width).astype(jnp.float32)
    shift_difference = previous.reshape(-1, width).astype(jnp.float32) - current_input
    shift_blended = (current_input + shift_difference * lag_blend_factor).astype(jnp.bfloat16)
    mixing_inner_all = jnp.tanh(
        jnp.dot(shift_blended, blending_lower_matrix, preferred_element_type=jnp.float32)
    ).astype(jnp.bfloat16)
    mixing_inner_width = blending_raise_matrix.shape[1]
    shift_mixed_rows = []
    for mix_component in range(5):
        mixing_inner_part = jnp.dot(
            mixing_inner_all[
                :, mix_component * mixing_inner_width : (mix_component + 1) * mixing_inner_width
            ],
            blending_raise_matrix[mix_component],
            preferred_element_type=jnp.float32,
        )
        shift_mixed_rows.append(
            (
                current_input
                + shift_difference * (constant_lag_blends[mix_component] + mixing_inner_part)
            ).astype(jnp.bfloat16)
        )
    return shift_mixed_rows


def wkv_blocks(
    acceptor_vectors,
    lookup_vectors,
    payload_vectors,
    logarithmic_fading_entries,
    diagonal_boost,
    starting_memory,
    approved_guesses,
):
    draft = acceptor_vectors.shape[1]
    cumulative = jnp.cumsum(logarithmic_fading_entries, axis=1)
    starts = jnp.concatenate(
        [jnp.zeros_like(logarithmic_fading_entries[:, :1]), cumulative], axis=1
    )
    before = starts[:, :draft]
    from_start = jnp.einsum(
        "bthi,bhij->bthj",
        acceptor_vectors * jnp.exp(before),
        starting_memory,
        precision=lax.Precision.HIGHEST,
    )
    later = jnp.arange(draft)[:, None] > jnp.arange(draft)[None, :]
    exponent = before[:, :, None] - cumulative[:, None, :]
    exponent = jnp.where(later[None, :, :, None, None], exponent, -1e30)
    scores = jnp.sum(
        acceptor_vectors[:, :, None] * lookup_vectors[:, None, :] * jnp.exp(exponent), axis=-1
    )
    inner = jnp.einsum("btsh,bshj->bthj", scores, payload_vectors, precision=lax.Precision.HIGHEST)
    diagonal_boost_contribution = (
        jnp.sum(acceptor_vectors * diagonal_boost * lookup_vectors, axis=-1, keepdims=True)
        * payload_vectors
    )
    outputs = from_start + inner + diagonal_boost_contribution
    at_accept = jnp.take_along_axis(starts, approved_guesses[:, None, None, None], axis=1)[:, 0]
    used = jnp.arange(draft)[None, :] < approved_guesses[:, None]
    coef_exp = jnp.where(used[:, :, None, None], at_accept[:, None] - cumulative, -1e30)
    weighted = jnp.exp(coef_exp) * lookup_vectors
    picked = jnp.exp(at_accept)[..., None] * starting_memory + jnp.einsum(
        "bshi,bshj->bhij", weighted, payload_vectors, precision=lax.Precision.HIGHEST
    )
    return (outputs, picked)


def gated_norm(outputs, gate_raw, gain, bias):
    centre = jnp.mean(outputs, axis=-1, keepdims=True)
    spread = outputs - centre
    variance = jnp.mean(spread * spread, axis=-1, keepdims=True)
    normed = (spread * lax.rsqrt(variance + norm_eps)).reshape(outputs.shape[0], -1)
    return ((normed * gain + bias) * jax.nn.silu(gate_raw)).astype(jnp.bfloat16)


def on_device(
    guess_vectors,
    preceding_symbol_vector,
    earlier_memory_matrix,
    lag_blend_factor,
    constant_lag_blends,
    blending_lower_matrix,
    blending_raise_matrix,
    constant_fading,
    fading_lower_matrix,
    fading_raise_matrix,
    diagonal_boost,
    acceptor_matrix,
    lookup_matrix,
    payload_matrix,
    gating_matrix,
    emission_matrix,
    groupwise_scaling_factor,
    groupwise_scaling_offset,
    usable_guess_amount,
    approved_guesses,
    destination_slot,
):
    own_reqs, draft, width = guess_vectors.shape
    group_count = lax.axis_size("mp")
    row_groups = lax.axis_size("dp")
    row_reqs = own_reqs * group_count
    row_index = lax.axis_index("dp")
    group_index = lax.axis_index("mp")
    local_width = acceptor_matrix.shape[1]
    local_heads = local_width // GROUP_DIMENSION
    gathered, edges_all = (
        lax.all_gather(guess_vectors, "mp", axis=0, tiled=True),
        lax.all_gather(preceding_symbol_vector, "mp", axis=0, tiled=True),
    )
    shift_mixed_rows = token_mixes(
        gathered,
        edges_all,
        lag_blend_factor,
        constant_lag_blends,
        blending_lower_matrix,
        blending_raise_matrix,
    )
    token_rows = row_reqs * draft
    sources = (shift_mixed_rows[3], shift_mixed_rows[1], shift_mixed_rows[2], shift_mixed_rows[4])
    pieces = (
        lax.all_gather(acceptor_matrix, "dp", axis=0, tiled=True),
        lax.all_gather(lookup_matrix, "dp", axis=0, tiled=True),
        lax.all_gather(payload_matrix, "dp", axis=0, tiled=True),
        lax.all_gather(gating_matrix, "dp", axis=0, tiled=True),
    )
    acceptor_vectors, lookup_vectors, payload_vectors, gate_raw = tuple(
        (
            jnp.dot(source_rows, piece, preferred_element_type=jnp.float32)
            for source_rows, piece in zip(sources, pieces)
        )
    )
    decay_inner_rows = jnp.tanh(
        jnp.dot(shift_mixed_rows[0], fading_lower_matrix, preferred_element_type=jnp.float32)
    ).astype(jnp.bfloat16)
    logarithmic_fading_entries = -jnp.exp(
        constant_fading
        + jnp.dot(decay_inner_rows, fading_raise_matrix, preferred_element_type=jnp.float32)
    )

    def to_heads(values):
        return values.reshape(row_reqs, draft, local_heads, GROUP_DIMENSION)

    row_accepted = lax.dynamic_slice_in_dim(approved_guesses, row_index * row_reqs, row_reqs)
    outputs, picked = wkv_blocks(
        to_heads(acceptor_vectors),
        to_heads(lookup_vectors),
        to_heads(payload_vectors),
        to_heads(logarithmic_fading_entries),
        diagonal_boost,
        earlier_memory_matrix,
        row_accepted,
    )
    hidden = gated_norm(
        outputs.reshape(token_rows, local_heads, GROUP_DIMENSION),
        gate_raw,
        groupwise_scaling_factor,
        groupwise_scaling_offset,
    )
    out_cols = lax.all_gather(emission_matrix, "dp", axis=1, tiled=True)
    attended = lax.psum_scatter(
        jnp.dot(hidden, out_cols, preferred_element_type=jnp.float32).astype(jnp.bfloat16),
        "mp",
        scatter_dimension=0,
        tiled=True,
    ).astype(jnp.float32)
    own_start = (row_index * group_count + group_index) * own_reqs
    own_lengths = lax.dynamic_slice_in_dim(usable_guess_amount, own_start, own_reqs)
    valid_mask = jnp.arange(draft, dtype=jnp.int32)[None, :] < own_lengths[:, None]
    layer_out = (
        guess_vectors.astype(jnp.float32)
        + jnp.where(
            valid_mask[..., None],
            attended.reshape(own_reqs, draft, width),
            jnp.zeros((), jnp.float32),
        )
    ).astype(jnp.bfloat16)
    edge_rows = jnp.concatenate([edges_all[:, None, :], gathered], axis=1)
    edge_cols = lax.dynamic_slice_in_dim(edge_rows, group_index * local_width, local_width, 2)
    chosen = jnp.take_along_axis(edge_cols, row_accepted[:, None, None], axis=1)[:, 0]
    capacity = 2 * row_reqs // row_groups
    target_rows = (destination_slot // row_reqs).reshape(row_groups, row_reqs)
    onehot = (
        target_rows[:, :, None] == jnp.arange(row_groups, dtype=jnp.int32)[None, None, :]
    ).astype(jnp.int32)
    earlier = jnp.cumsum(onehot, axis=1) - onehot
    ranks = jnp.sum(earlier * onehot, axis=-1)
    my_targets = lax.dynamic_index_in_dim(target_rows, row_index, 0, keepdims=False)
    my_ranks = lax.dynamic_index_in_dim(ranks, row_index, 0, keepdims=False)
    selected = (
        my_targets[:, None, None] == jnp.arange(row_groups, dtype=jnp.int32)[None, :, None]
    ) & (my_ranks[:, None, None] == jnp.arange(capacity, dtype=jnp.int32)[None, None, :])
    source_index = jnp.sum(
        selected.astype(jnp.int32) * jnp.arange(row_reqs, dtype=jnp.int32)[:, None, None], axis=0
    )
    filled = jnp.any(selected, axis=0)
    send_state = jnp.where(
        filled[..., None, None, None], picked[source_index], jnp.zeros((), jnp.float32)
    )
    send_edge = jnp.where(
        filled[..., None], chosen[source_index].astype(jnp.float32), jnp.zeros((), jnp.float32)
    )
    recv_state, recv_edge = (
        lax.all_to_all(
            send_state.astype(jnp.bfloat16), "dp", split_axis=0, concat_axis=0, tiled=True
        ).astype(send_state.dtype),
        lax.all_to_all(
            send_edge.astype(jnp.bfloat16), "dp", split_axis=0, concat_axis=0, tiled=True
        ).astype(send_edge.dtype),
    )
    wanted = row_index * row_reqs + jnp.arange(row_reqs, dtype=jnp.int32)
    total_reqs = destination_slot.shape[0]
    matches = (destination_slot[None, :] == wanted[:, None]).astype(jnp.int32)
    which = jnp.sum(matches * jnp.arange(total_reqs, dtype=jnp.int32)[None, :], axis=1)
    flat_index = which // row_reqs * capacity + ranks.reshape(-1)[which]
    next_state = recv_state.reshape(
        row_groups * capacity, local_heads, GROUP_DIMENSION, GROUP_DIMENSION
    )[flat_index]
    next_edge = recv_edge.reshape(row_groups * capacity, local_width)[flat_index].astype(
        jnp.bfloat16
    )
    return (layer_out, next_state, next_edge)


def solution(mesh):
    in_specs = (
        P(("dp", "mp"), None, None),
        P(("dp", "mp"), None),
        P("dp", "mp", None, None),
        P(),
        P(),
        P(),
        P(),
        P("mp"),
        P(),
        P(None, "mp"),
        P("mp", None),
        P("dp", "mp"),
        P("dp", "mp"),
        P("dp", "mp"),
        P("dp", "mp"),
        P("mp", "dp"),
        P("mp"),
        P("mp"),
        P(),
        P(),
        P(),
    )
    out_specs = (P(("dp", "mp"), None, None), P("dp", "mp", None, None), P("dp", "mp"))
    return jax.shard_map(
        on_device, mesh=mesh, in_specs=in_specs, out_specs=out_specs, check_vma=False
    )
```

profile of v0, /device:TPU:0, one launch (start us, length us, event | category | flops | bytes accessed | tf_op | source)
XLA Modules:
  0.0 585.9 jit_solution(18396825524794450216)
XLA Ops:
  7.3 0.7 all-gather.8.cloned.1.call-update
  8.0 0.7 all-gather.12.cloned.1.call-update
  8.8 0.7 all-gather.14.cloned.1.call-update
  9.5 0.5 all-gather.10.cloned.1.call-update
  10.1 0.5 all-gather.16.cloned.1.call-update
  10.7 0.5 all-gather.18.cloned.1.call-update
  11.6 0.2 select_reduce_fusion
  11.9 0.1 fusion.58
  12.1 0.2 and_reduce_fusion
  12.2 10.8 %all-gather = bf16[8,4,4096]{2,1,0:T(4,128)(2,1)S(1)} all-gather(bf16[1,4,4096]{2,1,0:T(4,128)(2,1)S(1)} %bitcast.122), channel_id=1, replica_groups=mesh['dp'=4,'mp'=8] {'mp'}, dimensions={0}, use_global_device_ids=true | all-gather | bytes 294912 | tf_op jit(solution)/shard_map/all_gather | solution.py:129
  23.1 0.5 copy.66
  23.9 25.6 %all-gather.8.cloned.1.call-done = bf16[32,16,4096]{2,1,0:T(8,128)(2,1)} async-done(((bf16[4,16,4096]{2,1,0:T(8,128)(2,1)}), bf16[32,16,4096]{2,1,0:T(8,128)(2,1)}) %all-gather.8.cloned.1.call-update) | async-done | bytes 4194320 | tf_op jit(solution)/shard_map/all_gather | solution.py:128
  49.4 3.7 pad_maximum_fusion
  53.1 1.9 copy-done.7
  55.1 2.0 fusion.28
  57.1 74.7 %all-gather.12.cloned.1.call-done = bf16[4096,512]{1,0:T(8,128)(2,1)} async-done(((bf16[1024,512]{1,0:T(8,128)(2,1)}), bf16[4096,512]{1,0:T(8,128)(2,1)}) %all-gather.12.cloned.1.call-update) | async-done | bytes 4194320 | tf_op jit(solution)/shard_map/all_gather | solution.py:144
  131.8 8.5 %fusion.23 = f32[512,512]{1,0:T(8,128)S(1)} fusion(bf16[4096,512]{1,0:T(8,128)(2,1)} %all-gather.12.cloned.1.call-done, bf16[512,4096]{1,0:T(8,128)(2,1)} %bitcast.105, bf16[512,4096]{1,0:T(8,128)(2,1)} %bitcast.112, f32[4096]{0:T(1024)S(1)} %bitcast.127, bf16[5,32,4096]{2,1,0:T(8,128)(2,1)} %param.27, bf16[512,160]{0,1:T(8,128)(2,1)S(1)} %fusion.28), kind=kOutput, calls=%fused_computation.48 | convolution fusion | flops 2296381440 | bytes 13942784 | tf_op jit(solution)/shard_map/dot_general | solution.py:149
  140.3 1.8 reshape.356
  142.2 70.5 %all-gather.14.cloned.1.call-done = bf16[4096,512]{1,0:T(8,128)(2,1)} async-done(((bf16[1024,512]{1,0:T(8,128)(2,1)}), bf16[4096,512]{1,0:T(8,128)(2,1)}) %all-gather.14.cloned.1.call-update) | async-done | bytes 4194320 | tf_op jit(solution)/shard_map/all_gather | solution.py:143
  212.7 8.6 %fusion.22 = f32[512,512]{1,0:T(8,128)S(1)} fusion(bf16[4096,512]{1,0:T(8,128)(2,1)} %all-gather.14.cloned.1.call-done, bf16[512,4096]{1,0:T(8,128)(2,1)} %bitcast.106, bf16[512,4096]{1,0:T(8,128)(2,1)} %bitcast.113, f32[4096]{0:T(1024)S(1)} %bitcast.126, bf16[5,32,4096]{2,1,0:T(8,128)(2,1)} %param.27, bf16[512,160]{0,1:T(8,128)(2,1)S(1)} %fusion.28), kind=kOutput, calls=%fused_computation.47 | convolution fusion | flops 2296381440 | bytes 13942784 | tf_op jit(solution)/shard_map/dot_general | solution.py:149
  221.3 1.8 mul.159
  223.1 6.9 %fusion.32 = bf16[512,64]{0,1:T(8,128)(2,1)S(1)} fusion(bf16[4096,64]{0,1:T(8,128)(2,1)S(1)} %copy-done.19, bf16[512,4096]{1,0:T(8,128)(2,1)} %bitcast.107, bf16[512,4096]{1,0:T(8,128)(2,1)} %bitcast.114, f32[4096]{0:T(1024)S(1)} %bitcast.125, bf16[5,32,4096]{2,1,0:T(8,128)(2,1)} %param.27, bf16[512,160]{0,1:T(8,128)(2,1)S(1)} %fusion.28), kind=kOutput, calls=%fused_computation.53 | convolution fusion | flops 417366016 | bytes 9289728 | tf_op jit(solution)/shard_map/dot_general | solution.py:154
  230.0 0.3 fusion.20
  230.4 1.9 reshape.355
  232.3 1.8 fusion.77
  234.1 59.4 %all-gather.10.cloned.1.call-done = bf16[4096,512]{1,0:T(8,128)(2,1)} async-done(((bf16[1024,512]{1,0:T(8,128)(2,1)}), bf16[4096,512]{1,0:T(8,128)(2,1)}) %all-gather.10.cloned.1.call-update) | async-done | bytes 4194320 | tf_op jit(solution)/shard_map/all_gather | solution.py:142
  293.4 8.6 %fusion.24 = f32[512,512]{1,0:T(8,128)S(1)} fusion(bf16[4096,512]{1,0:T(8,128)(2,1)} %all-gather.10.cloned.1.call-done, bf16[512,4096]{1,0:T(8,128)(2,1)} %bitcast.108, bf16[512,4096]{1,0:T(8,128)(2,1)} %bitcast.115, f32[4096]{0:T(1024)S(1)} %bitcast.124, bf16[5,32,4096]{2,1,0:T(8,128)(2,1)} %param.27, bf16[512,160]{0,1:T(8,128)(2,1)} %copy-done.25), kind=kOutput, calls=%fused_computation.49 | convolution fusion | flops 2296381440 | bytes 13942784 | tf_op jit(solution)/shard_map/dot_general | solution.py:149
  302.0 1.7 reshape.354
  303.8 1.5 concatenate.10
  305.3 2.2 gather_fusion.5
  307.7 6.3 %exponential_multiply_fusion = (f32[32,16,8,64]{3,2,1,0:T(8,128)}, f32[32,16,8,64]{3,2,1,0:T(8,128)}, f32[32,16,8]{2,1,0:T(8,128)S(1)}, f32[32,16,8,64]{3,2,1,0:T(8,128)}) fusion(f32[32,16,8,64]{3,2,1,0:T(8,128)} %mul.159, f32[32,16,8,64]{3,2,1,0:T(8,128)S(1)} %fusion.77, f32[32,8,64]{2,1,0:T(8,128)S(1)} %get-tuple-element.4, ...), kind=kLoop, calls=%fused_computation.35 | loop fusion | flops 1830912 | bytes 6375936 | tf_op jit(solution)/shard_map/mul | solution.py:81
  314.0 15.2 %multiply_reduce_fusion = f32[32,16,16,8]{3,2,1,0:T(8,128)} fusion(f32[32,16,8,64]{3,2,1,0:T(8,128)S(1)} %fusion.77, f32[32,16,8,64]{3,2,1,0:T(8,128)} %get-tuple-element.10, f32[32,16,8,64]{3,2,1,0:T(8,128)} %mul.159, f32[32,16,8,64]{3,2,1,0:T(8,128)} %reshape.354, pred[16,16]{1,0:T(8,128)(4,1)S(1)} %iota_compare_fusion.3), kind=kLoop, calls=%fused_computation.7 | loop fusion | flops 20905984 | bytes 4456704 | tf_op jit(solution)/shard_map/reduce_sum | solution.py:69
  329.3 4.0 copy.69
  333.3 10.2 %fusion.11 = f32[32,8,16,64]{3,2,1,0:T(8,128)S(1)} fusion(f32[32,8,64,64]{3,2,1,0:T(8,128)} %param.23, f32[32,16,8,64]{3,2,1,0:T(8,128)S(1)} %copy-done.6), kind=kOutput, calls=%fused_computation.33 | convolution fusion | flops 201326592 | bytes 6291456 | tf_op jit(solution)/shard_map/bthi,bhij->bthj/dot_general | solution.py:60
  343.5 3.6 fusion.76
  347.4 1.3 multiply_reduce_fusion.1
  348.9 4.5 copy.82
  353.5 0.7 gather_fusion.6
  354.2 19.7 %multiply_add_fusion = bf16[32,8,64,64]{3,2,1,0:T(8,128)(2,1)} fusion(f32[32,8,64,64]{3,2,1,0:T(8,128)} %param.23, f32[32,8,64]{2,1,0:T(8,128)S(1)} %get-tuple-element.3, f32[32,16,8,64]{3,2,1,0:T(8,128)} %get-tuple-element.7, f32[32,16,8,64]{3,2,1,0:T(8,128)} %reshape.356), kind=kOutput, calls=%fused_computation.23 | convolution fusion | flops 204472320 | bytes 8454144 | tf_op jit(solution)/shard_map/bshi,bshj->bhij/dot_general | solution.py:82
  373.9 7.8 %gather_fusion = bf16[64,8,64,64]{3,2,1,0:T(8,128)(2,1)} fusion(bf16[32,8,64,64]{3,2,1,0:T(8,128)(2,1)} %multiply_add_fusion, s32[1024]{0:T(1024)S(1)} %pad_clamp_fusion.2), kind=kCustom, calls=%fused_computation | custom fusion | bytes 8388864 | tf_op jit(solution)/shard_map/gather | solution.py:218
  381.8 0.7 gather_fusion.3
  382.5 0.7 fusion.56
  383.2 3.5 all-to-all-start.1
  386.7 10.5 %select_convert_fusion = bf16[4,16,8,64,64]{4,3,2,1,0:T(8,128)(2,1)} fusion(bf16[4,16,8,64,64]{4,3,2,1,0:T(8,128)(2,1)} %bitcast.103, pred[4,16]{1,0:T(4,128)(4,1)S(1)} %and_reduce_fusion), kind=kLoop, calls=%fused_computation.15 | loop fusion | flops 2097152 | bytes 8388672 | tf_op jit(solution)/shard_map/convert_element_type | solution.py:225
  397.3 2.2 copy.72
  399.8 0.1 mul.169
  399.9 1.4 copy.79
  401.3 1.5 reshape.357
  403.0 0.3 copy.75
  403.4 9.7 %reshape.439 = bf16[4,2,262144]{2,1,0:T(2,128)(2,1)} reshape(bf16[4,16,8,64,64]{4,3,2,1,0:T(8,128)(2,1)} %select_convert_fusion) | data formatting | bytes 8388608
  413.1 5.1 all-to-all-start
  418.2 0.2 reduce-scatter.2.cloned.1.call-start
  418.5 9.7 %multiply_convert_fusion = bf16[512,512]{1,0:T(8,128)(2,1)} fusion(bf16[4096,512]{1,0:T(8,128)(2,1)} %all-gather.16.cloned.1.call-done, bf16[512,4096]{1,0:T(8,128)(2,1)} %bitcast.109, bf16[512,4096]{1,0:T(8,128)(2,1)} %bitcast.116, f32[4096]{0:T(1024)S(1)} %bitcast.123, f32[512,512]{1,0:T(8,128)S(1)} %copy-done.12, f32[512,512]{1,0:T(8,128)S(1)} %copy-done.11, ...), kind=kOutput, calls=%fused_computation.57 | convolution fusion | flops 2299002880 | bytes 16568320 | tf_op jit(solution)/shard_map/dot_general | solution.py:149
  428.2 67.7 %all-gather.18.cloned.1.call-done = bf16[512,4096]{1,0:T(8,128)(2,1)} async-done(((bf16[512,1024]{1,0:T(8,128)(2,1)}), bf16[512,4096]{1,0:T(8,128)(2,1)}) %all-gather.18.cloned.1.call-update) | async-done | bytes 4194320 | tf_op jit(solution)/shard_map/all_gather | solution.py:180
  495.9 6.7 %convolution_convert_fusion = bf16[512,4096]{1,0:T(8,128)(2,1)} fusion(bf16[512,512]{1,0:T(8,128)(2,1)} %multiply_convert_fusion, bf16[512,4096]{1,0:T(8,128)(2,1)} %all-gather.18.cloned.1.call-done), kind=kOutput, calls=%fused_computation.24 | convolution fusion | flops 2149580800 | bytes 8912896 | tf_op jit(solution)/shard_map/dot_general | solution.py:182
  502.7 0.5 copy-done.23
  503.4 0.2 select_reduce_fusion.1
  503.6 0.7 gather_fusion.1
  504.4 1.2 gather_fusion.4
  505.6 40.1 %all-to-all-done = bf16[4,2,262144]{2,1,0:T(2,128)(2,1)} async-done(((bf16[4,2,262144]{2,1,0:T(2,128)(2,1)}), bf16[4,2,262144]{2,1,0:T(2,128)(2,1)}, u32[]{:S(2)}, u32[]{:S(2)}) %all-to-all-start) | async-done | bytes 4194336 | tf_op jit(solution)/shard_map/all_to_all | solution.py:224
  545.7 9.3 %reshape.440 = bf16[4,16,8,64,64]{4,3,2,1,0:T(8,128)(2,1)} reshape(bf16[4,2,262144]{2,1,0:T(2,128)(2,1)} %all-to-all-done) | data formatting | bytes 8388608
  555.0 11.3 %bitcast_convert_fusion = f32[64,8,64,64]{3,2,1,0:T(8,128)} fusion(bf16[4,16,8,64,64]{4,3,2,1,0:T(8,128)(2,1)} %reshape.440), kind=kLoop, calls=%fused_computation.22 | loop fusion | flops 2097152 | bytes 12582912 | tf_op jit(solution)/shard_map/reshape | solution.py:236
  566.3 10.4 %gather_fusion.2 = f32[32,8,64,64]{3,2,1,0:T(8,128)} fusion(f32[64,8,64,64]{3,2,1,0:T(8,128)} %bitcast_convert_fusion, s32[1024]{0:T(1024)S(1)} %pad_clamp_fusion), kind=kCustom, calls=%fused_computation.2 | custom fusion | bytes 8388736 | tf_op jit(solution)/shard_map/gather | solution.py:236
  576.7 2.1 fusion.34
  (101 shorter events, 2.6 us)
Async XLA Ops:
  7.2 47.9 %copy-start = (bf16[4096,160]{0,1:T(8,128)(2,1)S(1)}, bf16[4096,160]{0,1:T(8,128)(2,1)}, u32[]{:S(2)}) copy-start(bf16[4096,160]{0,1:T(8,128)(2,1)} %param.26) | copy-start | bytes 3932164
  7.2 4.0 copy-start.18
  7.2 4.2 copy-start.24
  7.2 5.0 copy-start.15
  7.2 16.4 %copy-start.14 = (f32[5,4096]{1,0:T(8,128)S(1)}, f32[5,4096]{1,0:T(8,128)}, u32[]{:S(2)}) copy-start(f32[5,4096]{1,0:T(8,128)} %param.25) | copy-start | bytes 245764
  7.2 42.2 %all-gather.8.cloned.1.call-start = ((), (), s32[]{:S(2)}) async-start(), calls=%async_computation.3 | async-start | bytes 4718592 | tf_op jit(solution)/shard_map/all_gather | solution.py:128
  8.0 123.8 %all-gather.12.cloned.1.call-start = ((), (), s32[]{:S(2)}) async-start(), calls=%async_computation.5 | async-start | bytes 5242880 | tf_op jit(solution)/shard_map/all_gather | solution.py:144
  8.7 204.0 %all-gather.14.cloned.1.call-start = ((), (), s32[]{:S(2)}) async-start(), calls=%async_computation.6 | async-start | bytes 5242880 | tf_op jit(solution)/shard_map/all_gather | solution.py:143
  9.4 284.0 %all-gather.10.cloned.1.call-start = ((), (), s32[]{:S(2)}) async-start(), calls=%async_computation.4 | async-start | bytes 5242880 | tf_op jit(solution)/shard_map/all_gather | solution.py:142
  10.0 408.5 %all-gather.16.cloned.1.call-start = ((), (), s32[]{:S(2)}) async-start(), calls=%async_computation.7 | async-start | bytes 5242880 | tf_op jit(solution)/shard_map/all_gather | solution.py:145
  10.6 485.3 %all-gather.18.cloned.1.call-start = ((), (), s32[]{:S(2)}) async-start(), calls=%async_computation.8 | async-start | bytes 5242880 | tf_op jit(solution)/shard_map/all_gather | solution.py:180
  23.1 30.1 %copy-start.8 = (bf16[32,1,4096]{2,0,1:T(8,128)(2,1)}, bf16[32,1,4096]{2,0,1:T(8,128)(2,1)S(1)}, u32[]{:S(2)}) copy-start(bf16[32,1,4096]{2,0,1:T(8,128)(2,1)S(1)} %broadcast_in_dim.75) | copy-start | bytes 786436
  49.4 5.7 copy-start.3
  49.4 5.7 copy-start.20
  53.1 1.9 copy-start.7
  57.1 166.0 %copy-start.25 = (bf16[512,160]{0,1:T(8,128)(2,1)}, bf16[512,160]{0,1:T(8,128)(2,1)S(1)}, u32[]{:S(2)}) copy-start(bf16[512,160]{0,1:T(8,128)(2,1)S(1)} %fusion.28) | copy-start | bytes 491524
  212.7 10.4 %copy-start.19 = (bf16[4096,64]{0,1:T(8,128)(2,1)S(1)}, bf16[4096,64]{0,1:T(8,128)(2,1)}, u32[]{:S(2)}) copy-start(bf16[4096,64]{0,1:T(8,128)(2,1)} %param.29) | copy-start | bytes 1572868
  223.1 6.9 %copy-start.13 = (bf16[64,512]{1,0:T(8,128)(2,1)S(1)}, bf16[64,512]{1,0:T(8,128)(2,1)}, u32[]{:S(2)}) copy-start(bf16[64,512]{1,0:T(8,128)(2,1)} %param.30) | copy-start | bytes 196612
  223.1 6.9 %copy-start.17 = (f32[512]{0:T(512)S(1)}, f32[512]{0:T(512)}, u32[]{:S(2)}) copy-start(f32[512]{0:T(512)} %param.28) | copy-start | bytes 6148
  302.0 5.6 copy-start.16
  329.3 4.0 copy-start.6
  333.3 10.2 %copy-start.2 = (f32[32,16,8,64]{3,2,1,0:T(8,128)S(1)}, f32[32,16,8,64]{3,2,1,0:T(8,128)}, u32[]{:S(2)}) copy-start(f32[32,16,8,64]{3,2,1,0:T(8,128)} %reshape.356) | copy-start | bytes 3145732
  333.3 10.2 %copy-start.5 = (f32[32,16,16,8]{2,1,3,0:T(8,128)S(1)}, f32[32,16,16,8]{2,1,3,0:T(8,128)}, u32[]{:S(2)}) copy-start(f32[32,16,16,8]{2,1,3,0:T(8,128)} %copy.69) | copy-start | bytes 786436
  348.8 4.5 copy-start.9
  383.2 29.9 %all-to-all-start.1 = ((bf16[4,16,512]{2,1,0:T(8,128)(2,1)}), bf16[4,16,512]{2,1,0:T(8,128)(2,1)S(1)}, u32[]{:S(2)}, u32[]{:S(2)}) async-start(bf16[4,16,512]{2,1,0:T(8,128)(2,1)} %fusion.56), calls=%async_computation.2 | async-start | bytes 131072 | tf_op jit(solution)/shard_map/all_to_all | solution.py:227
  399.5 1.9 copy-start.4
  413.1 5.4 copy-start.11
  413.1 5.4 copy-start.12
  413.1 5.5 copy-start.21
  413.1 5.5 copy-start.22
  413.1 132.6 %all-to-all-start = ((bf16[4,2,262144]{2,1,0:T(2,128)(2,1)}), bf16[4,2,262144]{2,1,0:T(2,128)(2,1)}, u32[]{:S(2)}, u32[]{:S(2)}) async-start(bf16[4,2,262144]{2,1,0:T(2,128)(2,1)} %reshape.439), calls=%async_computation.1 | async-start | bytes 8388608 | tf_op jit(solution)/shard_map/all_to_all | solution.py:224
  418.2 158.5 %reduce-scatter.2.cloned.1.call-start = ((), (), s32[]{:S(2)}) async-start(), calls=%async_computation.9 | async-start | bytes 4718592 | tf_op jit(solution)/shard_map/reduce_scatter | solution.py:181
  502.6 0.7 copy-start.23
  566.3 10.4 %copy-start.10 = (bf16[4,16,4096]{2,1,0:T(8,128)(2,1)S(1)}, bf16[4,16,4096]{2,1,0:T(8,128)(2,1)}, u32[]{:S(2)}) copy-start(bf16[4,16,4096]{2,1,0:T(8,128)(2,1)} %param.21) | copy-start | bytes 1572868
  566.3 12.5 %copy-start.1 = (bf16[4096,160]{0,1:T(8,128)(2,1)S(1)}, bf16[4096,160]{0,1:T(8,128)(2,1)}, u32[]{:S(2)}) copy-start(bf16[4096,160]{0,1:T(8,128)(2,1)} %param.26) | copy-start | bytes 3932164
Sparse Core Ops, SparseCore 0:
  9.9 39.4 all-gather.7
  51.0 80.7 all-gather.11
  133.4 79.2 all-gather.13
  214.1 79.2 all-gather.9
  294.9 79.2 all-gather.15
  375.6 120.2 all-gather.17
  502.8 49.4 reduce-scatter.1
where the time goes:
time: 590 us; the launch traced here: 586 us
  waiting for transfers between devices  342 us (58%)
  matrix products  84.8 us (14%)
  local copies, waits for them, and re-layouts  70.2 us (12%)
  other arithmetic  54.3 us (9%)
  between operations  15 us (3%)
  blocking collectives  10.8 us (2%)
  starting transfers between devices  9.1 us (2%)
    all_gather x1, waiting for transfers between devices, on_device(): lax.all_gather(payload_matrix, 'dp', axis=0, tiled=True)  74.7 us
    all_gather x1, waiting for transfers between devices, on_device(): lax.all_gather(lookup_matrix, 'dp', axis=0, tiled=True)  70.5 us
    all_gather x1, waiting for transfers between devices, on_device(): out_cols = lax.all_gather(emission_matrix, 'dp', axis=1, tiled=True)  67.7 us
    all_gather x1, waiting for transfers between devices, on_device(): lax.all_gather(acceptor_matrix, 'dp', axis=0, tiled=True)  59.4 us
    all_to_all x1, waiting for transfers between devices, on_device(): lax.all_to_all(send_state.astype(jnp.bfloat16), 'dp', split_axis=0, conca...  40.1 us
    dot_general x4, matrix products, on_device(): jnp.dot(source_rows, piece, preferred_element_type=jnp.float32)  35.4 us
    all_gather x1, waiting for transfers between devices, on_device(): lax.all_gather(guess_vectors, 'mp', axis=0, tiled=True)  25.6 us
    unnamed x55, local copies, waits for them, and re-layouts  21.5 us
  transfers between devices with their start and end apart: 9, of which 6 were waited for; matrix products, arithmetic and copies ran while one was open for 35% of the time, Pallas kernels for 0%

commit v1 on v0

--- a/solution.py
+++ b/solution.py
@@ -177,7 +177,12 @@
         groupwise_scaling_factor,
         groupwise_scaling_offset,
     )
-    out_cols = lax.all_gather(emission_matrix, "dp", axis=1, tiled=True)
+    ring = [emission_matrix]
+    for hop in range(3):
+        ring.append(lax.ppermute(ring[-1], "dp", [(dev, (dev + 1) % 4) for dev in range(4)]))
+    out_cols = jnp.roll(
+        jnp.concatenate(ring[::-1], axis=1), (lax.axis_index("dp") + 1) * ring[0].shape[1], axis=1
+    )
     attended = lax.psum_scatter(
         jnp.dot(hidden, out_cols, preferred_element_type=jnp.float32).astype(jnp.bfloat16),
         "mp",

time: 590 us -> 550 us (0.932)
  waiting for transfers between devices: 342 us -> 285 us
  local copies, waits for them, and re-layouts: 70.2 us -> 86.5 us
    ppermute x0 -> x3, waiting for transfers between devices: none -> 85.4 us  [on_device(): lax.ppermute(ring[-1], 'dp', [(dev, (dev + 1) % 4) for dev in range(4)])]
    all_gather x1 -> x0, waiting for transfers between devices: 67.7 us -> none  [on_device(): out_cols = lax.all_gather(emission_matrix, 'dp', axis=1, tiled=True)]
    all_gather x1, waiting for transfers between devices: 59.4 us -> 9.76 us  [on_device(): lax.all_gather(acceptor_matrix, 'dp', axis=0, tiled=True)]
    all_to_all x1, waiting for transfers between devices: 40.1 us -> 73.8 us  [on_device(): lax.all_to_all(send_state.astype(jnp.bfloat16), 'dp', split_axis=0, conca...]
    all_gather x1, waiting for transfers between devices: 74.7 us -> 43 us  [on_device(): lax.all_gather(payload_matrix, 'dp', axis=0, tiled=True)]
    all_gather x1, waiting for transfers between devices: 25.6 us -> 0.01 us  [on_device(): lax.all_gather(guess_vectors, 'mp', axis=0, tiled=True)]
    unnamed x55 -> x58, local copies, waits for them, and re-layouts: 21.5 us -> 32.2 us
  transfers between devices with their start and end apart: 9 -> 11, of which waited for: 6 -> 7; matrix products, arithmetic and copies ran while one was open for 35% -> 40% of each run, Pallas kernels for 0% -> 0%
where the time goes in v1:
time: 550 us; the launch traced here: 546 us
  waiting for transfers between devices  285 us (52%)
  local copies, waits for them, and re-layouts  86.5 us (16%)
  matrix products  84.9 us (15%)
  other arithmetic  52.1 us (9%)
  between operations  15 us (3%)
  starting transfers between devices  12.2 us (2%)
  blocking collectives  10.5 us (2%)
    ppermute x3, waiting for transfers between devices, on_device(): lax.ppermute(ring[-1], 'dp', [(dev, (dev + 1) % 4) for dev in range(4)])  85.4 us
    all_to_all x1, waiting for transfers between devices, on_device(): lax.all_to_all(send_state.astype(jnp.bfloat16), 'dp', split_axis=0, conca...  73.8 us
    all_gather x1, waiting for transfers between devices, on_device(): lax.all_gather(lookup_matrix, 'dp', axis=0, tiled=True)  70.1 us
    all_gather x1, waiting for transfers between devices, on_device(): lax.all_gather(payload_matrix, 'dp', axis=0, tiled=True)  43 us
    dot_general x4, matrix products, on_device(): jnp.dot(source_rows, piece, preferred_element_type=jnp.float32)  35.5 us
    unnamed x58, local copies, waits for them, and re-layouts  32.2 us
    dot_general x1, matrix products, wkv_blocks(): jnp.einsum('bshi,bshj->bhij', weighted, payload_vectors, precision=lax.Pr...  19.7 us
    reduce_sum x1, other arithmetic, wkv_blocks(): jnp.sum(acceptor_vectors[:, :, None] * lookup_vectors[:, None, :] * jnp.e...  13.1 us
  transfers between devices with their start and end apart: 11, of which 7 were waited for; matrix products, arithmetic and copies ran while one was open for 40% of the time, Pallas kernels for 0%

profile of v1, /device:TPU:0, one launch (start us, length us, event | category | flops | bytes accessed | tf_op | source)
XLA Modules:
  0.0 545.9 jit_solution(14952629670545273738)
XLA Ops:
  7.2 0.7 all-gather.7.cloned.1.call-update
  8.0 0.7 all-gather.9.cloned.1.call-update
  8.7 0.7 all-gather.13.cloned.1.call-update
  10.0 3.1 collective-permute-start
  13.9 24.6 %collective-permute-done = bf16[512,1024]{1,0:T(8,128)(2,1)S(1)} collective-permute-done((bf16[512,1024]{1,0:T(8,128)(2,1)}, bf16[512,1024]{1,0:T(8,128)(2,1)S(1)}, u32[]{:S(2)}, u32[]{:S(2)}) %collective-permute-start) | collective-permute-done | bytes 1048608 | tf_op jit(solution)/shard_map/ppermute | solution.py:182
  38.8 27.7 %collective-permute-done.1 = bf16[512,1024]{1,0:T(8,128)(2,1)} collective-permute-done((bf16[512,1024]{1,0:T(8,128)(2,1)S(1)}, bf16[512,1024]{1,0:T(8,128)(2,1)}, u32[]{:S(2)}, u32[]{:S(2)}) %collective-permute-start.1) | collective-permute-done | bytes 1048608 | tf_op jit(solution)/shard_map/ppermute | solution.py:182
  66.5 10.5 %all-gather = bf16[8,4,4096]{2,1,0:T(4,128)(2,1)} all-gather(bf16[1,4,4096]{2,1,0:T(4,128)(2,1)} %bitcast.121), channel_id=1, replica_groups=mesh['dp'=4,'mp'=8] {'mp'}, dimensions={0}, use_global_device_ids=true | all-gather | bytes 294912 | tf_op jit(solution)/shard_map/all_gather | solution.py:129
  77.0 1.7 broadcast_in_dim.75
  78.7 2.3 copy.66
  81.2 1.3 fusion.77
  82.5 33.1 %collective-permute-done.2 = bf16[512,1024]{1,0:T(8,128)(2,1)} collective-permute-done((bf16[512,1024]{1,0:T(8,128)(2,1)}, bf16[512,1024]{1,0:T(8,128)(2,1)}, u32[]{:S(2)}, u32[]{:S(2)}) %collective-permute-start.2) | collective-permute-done | bytes 1048608 | tf_op jit(solution)/shard_map/ppermute | solution.py:182
  115.6 2.3 constant_dynamic-update-slice_fusion.7
  117.9 2.3 constant_dynamic-update-slice_fusion.6
  120.2 1.0 constant_dynamic-update-slice_fusion.5
  121.2 1.0 constant_dynamic-update-slice_fusion.4
  122.2 2.3 constant_dynamic-update-slice_fusion.3
  124.5 2.3 constant_dynamic-update-slice_fusion.2
  126.8 1.0 constant_dynamic-update-slice_fusion.1
  127.8 1.0 constant_dynamic-update-slice_fusion
  128.9 3.7 pad_maximum_fusion
  132.6 2.0 fusion.29
  134.7 7.0 %fusion.33 = bf16[512,64]{0,1:T(8,128)(2,1)S(1)} fusion(bf16[4096,64]{0,1:T(8,128)(2,1)S(1)} %copy-done.17, bf16[512,4096]{1,0:T(8,128)(2,1)} %bitcast.104, bf16[512,4096]{1,0:T(8,128)(2,1)} %bitcast.111, f32[4096]{0:T(1024)S(1)} %bitcast.126, bf16[5,32,4096]{2,1,0:T(8,128)(2,1)} %param.27, bf16[512,160]{0,1:T(8,128)(2,1)S(1)} %fusion.29), kind=kOutput, calls=%fused_computation.54 | convolution fusion | flops 417366016 | bytes 9289728 | tf_op jit(solution)/shard_map/dot_general | solution.py:154
  142.0 1.7 reshape.355
  143.7 1.7 fusion.79
  145.5 9.8 %all-gather.9.cloned.1.call-done = bf16[4096,512]{1,0:T(8,128)(2,1)} async-done(((bf16[1024,512]{1,0:T(8,128)(2,1)}), bf16[4096,512]{1,0:T(8,128)(2,1)}) %all-gather.9.cloned.1.call-update) | async-done | bytes 4194320 | tf_op jit(solution)/shard_map/all_gather | solution.py:142
  155.2 8.6 %fusion.25 = f32[512,512]{1,0:T(8,128)S(1)} fusion(bf16[4096,512]{1,0:T(8,128)(2,1)} %all-gather.9.cloned.1.call-done, bf16[512,4096]{1,0:T(8,128)(2,1)} %bitcast.105, bf16[512,4096]{1,0:T(8,128)(2,1)} %bitcast.112, f32[4096]{0:T(1024)S(1)} %bitcast.125, bf16[5,32,4096]{2,1,0:T(8,128)(2,1)} %param.27, bf16[512,160]{0,1:T(8,128)(2,1)} %copy-done.23), kind=kOutput, calls=%fused_computation.50 | convolution fusion | flops 2296381440 | bytes 13942784 | tf_op jit(solution)/shard_map/dot_general | solution.py:149
  163.8 1.7 reshape.354
  165.5 70.1 %all-gather.13.cloned.1.call-done = bf16[4096,512]{1,0:T(8,128)(2,1)} async-done(((bf16[1024,512]{1,0:T(8,128)(2,1)}), bf16[4096,512]{1,0:T(8,128)(2,1)}) %all-gather.13.cloned.1.call-update) | async-done | bytes 4194320 | tf_op jit(solution)/shard_map/all_gather | solution.py:143
  235.7 8.7 %fusion.23 = f32[512,512]{1,0:T(8,128)S(1)} fusion(bf16[4096,512]{1,0:T(8,128)(2,1)} %all-gather.13.cloned.1.call-done, bf16[512,4096]{1,0:T(8,128)(2,1)} %bitcast.106, bf16[512,4096]{1,0:T(8,128)(2,1)} %bitcast.113, f32[4096]{0:T(1024)S(1)} %bitcast.124, bf16[5,32,4096]{2,1,0:T(8,128)(2,1)} %param.27, bf16[512,160]{0,1:T(8,128)(2,1)} %copy-done.23), kind=kOutput, calls=%fused_computation.48 | convolution fusion | flops 2296381440 | bytes 13942784 | tf_op jit(solution)/shard_map/dot_general | solution.py:149
  244.4 1.7 mul.162
  246.1 1.6 concatenate.16
  247.7 2.2 gather_fusion.5
  250.1 6.3 %exponential_multiply_fusion = (f32[32,16,8,64]{3,2,1,0:T(8,128)}, f32[32,16,8,64]{3,2,1,0:T(8,128)}, f32[32,16,8]{2,1,0:T(8,128)S(1)}, f32[32,16,8,64]{3,2,1,0:T(8,128)S(1)}) fusion(f32[32,16,8,64]{3,2,1,0:T(8,128)} %mul.162, f32[32,16,8,64]{3,2,1,0:T(8,128)S(1)} %fusion.79, f32[32,8,64]{2,1,0:T(8,128)S(1)} %get-tuple-element.4, ...), kind=kLoop, calls=%fused_computation.36 | loop fusion | flops 1830912 | bytes 6375936 | tf_op jit(solution)/shard_map/mul | solution.py:81
  256.4 13.1 %multiply_reduce_fusion = f32[32,16,16,8]{3,2,1,0:T(8,128)} fusion(f32[32,16,8,64]{3,2,1,0:T(8,128)S(1)} %fusion.79, f32[32,16,8,64]{3,2,1,0:T(8,128)S(1)} %get-tuple-element.10, f32[32,16,8,64]{3,2,1,0:T(8,128)S(1)} %copy-done.3, f32[32,16,8,64]{3,2,1,0:T(8,128)S(1)} %copy-done.2, pred[16,16]{1,0:T(8,128)(4,1)S(1)} %iota_compare_fusion.3), kind=kLoop, calls=%fused_computation.7 | loop fusion | flops 20905984 | bytes 4456704 | tf_op jit(solution)/shard_map/reduce_sum | solution.py:69
  269.5 3.8 copy.69
  273.4 43.0 %all-gather.11.cloned.1.call-done = bf16[4096,512]{1,0:T(8,128)(2,1)} async-done(((bf16[1024,512]{1,0:T(8,128)(2,1)}), bf16[4096,512]{1,0:T(8,128)(2,1)}) %all-gather.11.cloned.1.call-update) | async-done | bytes 4194320 | tf_op jit(solution)/shard_map/all_gather | solution.py:144
  316.4 8.6 %fusion.24 = f32[512,512]{1,0:T(8,128)S(1)} fusion(bf16[4096,512]{1,0:T(8,128)(2,1)} %all-gather.11.cloned.1.call-done, bf16[512,4096]{1,0:T(8,128)(2,1)} %bitcast.107, bf16[512,4096]{1,0:T(8,128)(2,1)} %bitcast.114, f32[4096]{0:T(1024)S(1)} %bitcast.123, bf16[5,32,4096]{2,1,0:T(8,128)(2,1)} %param.27, bf16[512,160]{0,1:T(8,128)(2,1)} %copy-done.23), kind=kOutput, calls=%fused_computation.49 | convolution fusion | flops 2296381440 | bytes 13942784 | tf_op jit(solution)/shard_map/dot_general | solution.py:149
  325.0 1.8 reshape.356
  326.8 0.6 copy-done.7
  327.3 10.2 %fusion.12 = f32[32,8,16,64]{3,2,1,0:T(8,128)S(1)} fusion(f32[32,8,64,64]{3,2,1,0:T(8,128)} %param.23, f32[32,16,8,64]{3,2,1,0:T(8,128)S(1)} %copy-done.7), kind=kOutput, calls=%fused_computation.34 | convolution fusion | flops 201326592 | bytes 6291456 | tf_op jit(solution)/shard_map/bthi,bhij->bthj/dot_general | solution.py:60
  337.6 3.6 fusion.78
  341.4 1.3 multiply_reduce_fusion.1
  342.9 4.6 copy.82
  347.5 0.7 gather_fusion.6
  348.3 19.7 %multiply_add_fusion = bf16[32,8,64,64]{3,2,1,0:T(8,128)(2,1)} fusion(f32[32,8,64,64]{3,2,1,0:T(8,128)} %param.23, f32[32,8,64]{2,1,0:T(8,128)S(1)} %get-tuple-element.3, f32[32,16,8,64]{3,2,1,0:T(8,128)} %get-tuple-element.7, f32[32,16,8,64]{3,2,1,0:T(8,128)} %reshape.356), kind=kOutput, calls=%fused_computation.23 | convolution fusion | flops 204472320 | bytes 8454144 | tf_op jit(solution)/shard_map/bshi,bshj->bhij/dot_general | solution.py:82
  368.0 7.6 %gather_fusion = bf16[64,8,64,64]{3,2,1,0:T(8,128)(2,1)} fusion(bf16[32,8,64,64]{3,2,1,0:T(8,128)(2,1)} %multiply_add_fusion, s32[1024]{0:T(1024)S(1)} %pad_clamp_fusion.2), kind=kCustom, calls=%fused_computation | custom fusion | bytes 8388864 | tf_op jit(solution)/shard_map/gather | solution.py:223
  375.7 0.7 gather_fusion.3
  376.4 0.7 fusion.57
  377.1 3.5 all-to-all-start.1
  380.6 10.4 %select_convert_fusion = bf16[4,16,8,64,64]{4,3,2,1,0:T(8,128)(2,1)} fusion(bf16[4,16,8,64,64]{4,3,2,1,0:T(8,128)(2,1)} %bitcast.102, pred[4,16]{1,0:T(4,128)(4,1)S(1)} %and_reduce_fusion), kind=kLoop, calls=%fused_computation.15 | loop fusion | flops 2097152 | bytes 8388672 | tf_op jit(solution)/shard_map/convert_element_type | solution.py:230
  391.0 2.3 copy.72
  393.4 1.9 reshape.357
  396.3 1.4 copy.75
  397.7 9.5 %reshape.439 = bf16[4,2,262144]{2,1,0:T(2,128)(2,1)} reshape(bf16[4,16,8,64,64]{4,3,2,1,0:T(8,128)(2,1)} %select_convert_fusion) | data formatting | bytes 8388608
  407.2 5.2 all-to-all-start
  412.7 9.6 %multiply_convert_fusion = bf16[512,512]{1,0:T(8,128)(2,1)} fusion(bf16[4096,512]{1,0:T(8,128)(2,1)} %all-gather.15.cloned.1.call-done, bf16[512,4096]{1,0:T(8,128)(2,1)} %bitcast.108, bf16[512,4096]{1,0:T(8,128)(2,1)} %bitcast.115, f32[4096]{0:T(1024)S(1)} %bitcast.122, f32[512,512]{1,0:T(8,128)S(1)} %copy.79, f32[512,512]{1,0:T(8,128)S(1)} %reshape.357, ...), kind=kOutput, calls=%fused_computation.58 | convolution fusion | flops 2299002880 | bytes 16568320 | tf_op jit(solution)/shard_map/dot_general | solution.py:149
  422.3 6.6 %convolution_convert_fusion = bf16[512,4096]{1,0:T(8,128)(2,1)} fusion(bf16[512,512]{1,0:T(8,128)(2,1)} %multiply_convert_fusion, bf16[512,8192]{1,0:T(8,128)(2,1)} %constant_dynamic-update-slice_fusion, s32[]{:T(128)S(6)} %select_n.128), kind=kOutput, calls=%fused_computation.24 | convolution fusion | flops 2149580800 | bytes 8912900 | tf_op jit(solution)/shard_map/dot_general | solution.py:187
  429.9 0.7 gather_fusion.1
  430.7 1.2 gather_fusion.4
  431.9 73.8 %all-to-all-done = bf16[4,2,262144]{2,1,0:T(2,128)(2,1)} async-done(((bf16[4,2,262144]{2,1,0:T(2,128)(2,1)}), bf16[4,2,262144]{2,1,0:T(2,128)(2,1)}, u32[]{:S(2)}, u32[]{:S(2)}) %all-to-all-start) | async-done | bytes 4194336 | tf_op jit(solution)/shard_map/all_to_all | solution.py:229
  505.7 9.3 %reshape.440 = bf16[4,16,8,64,64]{4,3,2,1,0:T(8,128)(2,1)} reshape(bf16[4,2,262144]{2,1,0:T(2,128)(2,1)} %all-to-all-done) | data formatting | bytes 8388608
  515.0 11.3 %bitcast_convert_fusion = f32[64,8,64,64]{3,2,1,0:T(8,128)} fusion(bf16[4,16,8,64,64]{4,3,2,1,0:T(8,128)(2,1)} %reshape.440), kind=kLoop, calls=%fused_computation.22 | loop fusion | flops 2097152 | bytes 12582912 | tf_op jit(solution)/shard_map/reshape | solution.py:241
  526.3 10.4 %gather_fusion.2 = f32[32,8,64,64]{3,2,1,0:T(8,128)} fusion(f32[64,8,64,64]{3,2,1,0:T(8,128)} %bitcast_convert_fusion, s32[1024]{0:T(1024)S(1)} %pad_clamp_fusion), kind=kCustom, calls=%fused_computation.2 | custom fusion | bytes 8388736 | tf_op jit(solution)/shard_map/gather | solution.py:241
  536.7 2.1 fusion.35
  (108 shorter events, 5.2 us)
Async XLA Ops:
  7.2 125.4 %copy-start = (bf16[4096,160]{0,1:T(8,128)(2,1)S(1)}, bf16[4096,160]{0,1:T(8,128)(2,1)}, u32[]{:S(2)}) copy-start(bf16[4096,160]{0,1:T(8,128)(2,1)} %param.26) | copy-start | bytes 3932164
  7.2 6.0 %copy-start.22 = (s32[128]{0:T(128)S(1)}, s32[128]{0:T(128)}, u32[]{:S(2)}) copy-start(s32[128]{0:T(128)} %param.41) | copy-start | bytes 1540
  7.2 31.3 %copy-start.16 = (s32[128]{0:T(128)S(1)}, s32[128]{0:T(128)}, u32[]{:S(2)}) copy-start(s32[128]{0:T(128)} %param.40) | copy-start | bytes 1540
  7.2 121.7 %all-gather.7.cloned.1.call-start = ((), (), s32[]{:S(2)}) async-start(), calls=%async_computation.3 | async-start | bytes 4718592 | tf_op jit(solution)/shard_map/all_gather | solution.py:128
  7.9 147.3 %all-gather.9.cloned.1.call-start = ((), (), s32[]{:S(2)}) async-start(), calls=%async_computation.4 | async-start | bytes 5242880 | tf_op jit(solution)/shard_map/all_gather | solution.py:142
  8.7 227.0 %all-gather.13.cloned.1.call-start = ((), (), s32[]{:S(2)}) async-start(), calls=%async_computation.6 | async-start | bytes 5242880 | tf_op jit(solution)/shard_map/all_gather | solution.py:143
  9.4 307.0 %all-gather.11.cloned.1.call-start = ((), (), s32[]{:S(2)}) async-start(), calls=%async_computation.5 | async-start | bytes 5242880 | tf_op jit(solution)/shard_map/all_gather | solution.py:144
  10.0 402.7 %all-gather.15.cloned.1.call-start = ((), (), s32[]{:S(2)}) async-start(), calls=%async_computation.7 | async-start | bytes 5242880 | tf_op jit(solution)/shard_map/all_gather | solution.py:145
  10.0 28.5 %collective-permute-start = (bf16[512,1024]{1,0:T(8,128)(2,1)}, bf16[512,1024]{1,0:T(8,128)(2,1)S(1)}, u32[]{:S(2)}, u32[]{:S(2)}) collective-permute-start(bf16[512,1024]{1,0:T(8,128)(2,1)} %param.36), channel_id=1, source_target_pairs={{0,8},{8,16},{16,24},{24,0},{1,9},{9,17},{17,25},{25,1},{2,10},{10... | collective-permute-start | bytes 3145736 | tf_op jit(solution)/shard_map/ppermute | solution.py:182
  13.3 107.9 %copy-start.9 = (bf16[512,1024]{1,0:T(8,128)(2,1)S(1)}, bf16[512,1024]{1,0:T(8,128)(2,1)}, u32[]{:S(2)}) copy-start(bf16[512,1024]{1,0:T(8,128)(2,1)} %param.36) | copy-start | bytes 3145732
  38.5 28.0 %collective-permute-start.1 = (bf16[512,1024]{1,0:T(8,128)(2,1)S(1)}, bf16[512,1024]{1,0:T(8,128)(2,1)}, u32[]{:S(2)}, u32[]{:S(2)}) collective-permute-start(bf16[512,1024]{1,0:T(8,128)(2,1)S(1)} %collective-permute-done), channel_id=1, source_target_pairs={{0,8},{8,16},{16,24},{24,0},{1,9},{9,17},{17,25},{25,1},{2,10},{10... | collective-permute-start | bytes 3145736 | tf_op jit(solution)/shard_map/ppermute | solution.py:182
  66.5 49.1 %collective-permute-start.2 = (bf16[512,1024]{1,0:T(8,128)(2,1)}, bf16[512,1024]{1,0:T(8,128)(2,1)}, u32[]{:S(2)}, u32[]{:S(2)}) collective-permute-start(bf16[512,1024]{1,0:T(8,128)(2,1)} %collective-permute-done.1), channel_id=1, source_target_pairs={{0,8},{8,16},{16,24},{24,0},{1,9},{9,17},{17,25},{25,1},{2,10},{10... | collective-permute-start | bytes 3145736 | tf_op jit(solution)/shard_map/ppermute | solution.py:182
  128.9 3.7 copy-start.5
  128.9 3.7 copy-start.18
  132.6 2.0 copy-start.8
  132.6 2.0 copy-start.17
  134.6 7.0 %copy-start.23 = (bf16[512,160]{0,1:T(8,128)(2,1)}, bf16[512,160]{0,1:T(8,128)(2,1)S(1)}, u32[]{:S(2)}) copy-start(bf16[512,160]{0,1:T(8,128)(2,1)S(1)} %fusion.29) | copy-start | bytes 491524
  134.6 7.0 %copy-start.13 = (bf16[64,512]{1,0:T(8,128)(2,1)S(1)}, bf16[64,512]{1,0:T(8,128)(2,1)}, u32[]{:S(2)}) copy-start(bf16[64,512]{1,0:T(8,128)(2,1)} %param.30) | copy-start | bytes 196612
  134.6 7.0 %copy-start.15 = (f32[512]{0:T(512)S(1)}, f32[512]{0:T(512)}, u32[]{:S(2)}) copy-start(f32[512]{0:T(512)} %param.28) | copy-start | bytes 6148
  244.4 5.7 %copy-start.14 = (f32[8,64]{1,0:T(8,128)S(1)}, f32[8,64]{1,0:T(8,128)}, u32[]{:S(2)}) copy-start(f32[8,64]{1,0:T(8,128)} %param.31) | copy-start | bytes 6148
  250.1 6.3 %copy-start.2 = (f32[32,16,8,64]{3,2,1,0:T(8,128)S(1)}, f32[32,16,8,64]{3,2,1,0:T(8,128)}, u32[]{:S(2)}) copy-start(f32[32,16,8,64]{3,2,1,0:T(8,128)} %reshape.354) | copy-start | bytes 3145732
  250.1 6.3 %copy-start.3 = (f32[32,16,8,64]{3,2,1,0:T(8,128)S(1)}, f32[32,16,8,64]{3,2,1,0:T(8,128)}, u32[]{:S(2)}) copy-start(f32[32,16,8,64]{3,2,1,0:T(8,128)} %mul.162) | copy-start | bytes 3145732
  325.0 2.4 copy-start.7
  327.3 10.2 %copy-start.4 = (f32[32,16,8,64]{3,2,1,0:T(8,128)S(1)}, f32[32,16,8,64]{3,2,1,0:T(8,128)}, u32[]{:S(2)}) copy-start(f32[32,16,8,64]{3,2,1,0:T(8,128)} %reshape.356) | copy-start | bytes 3145732
  327.3 10.2 %copy-start.6 = (f32[32,16,16,8]{2,1,3,0:T(8,128)S(1)}, f32[32,16,16,8]{2,1,3,0:T(8,128)}, u32[]{:S(2)}) copy-start(f32[32,16,16,8]{2,1,3,0:T(8,128)} %copy.69) | copy-start | bytes 786436
  342.9 4.6 copy-start.10
  377.1 30.1 %all-to-all-start.1 = ((bf16[4,16,512]{2,1,0:T(8,128)(2,1)}), bf16[4,16,512]{2,1,0:T(8,128)(2,1)S(1)}, u32[]{:S(2)}, u32[]{:S(2)}) async-start(bf16[4,16,512]{2,1,0:T(8,128)(2,1)} %fusion.57), calls=%async_computation.2 | async-start | bytes 131072 | tf_op jit(solution)/shard_map/all_to_all | solution.py:232
  407.2 5.5 %copy-start.12 = (f32[512,512]{1,0:T(8,128)S(1)}, f32[512,512]{1,0:T(8,128)}, u32[]{:S(2)}) copy-start(f32[512,512]{1,0:T(8,128)} %copy.75) | copy-start | bytes 3145732
  407.2 5.5 %copy-start.19 = (f32[512]{0:T(512)S(1)}, f32[512]{0:T(512)}, u32[]{:S(2)}) copy-start(f32[512]{0:T(512)} %param.38) | copy-start | bytes 6148
  407.2 5.5 %copy-start.20 = (f32[512]{0:T(512)S(1)}, f32[512]{0:T(512)}, u32[]{:S(2)}) copy-start(f32[512]{0:T(512)} %param.37) | copy-start | bytes 6148
  407.2 98.5 %all-to-all-start = ((bf16[4,2,262144]{2,1,0:T(2,128)(2,1)}), bf16[4,2,262144]{2,1,0:T(2,128)(2,1)}, u32[]{:S(2)}, u32[]{:S(2)}) async-start(bf16[4,2,262144]{2,1,0:T(2,128)(2,1)} %reshape.439), calls=%async_computation.1 | async-start | bytes 8388608 | tf_op jit(solution)/shard_map/all_to_all | solution.py:229
  412.4 124.3 %reduce-scatter.2.cloned.1.call-start = ((), (), s32[]{:S(2)}) async-start(), calls=%async_computation.8 | async-start | bytes 4718592 | tf_op jit(solution)/shard_map/reduce_scatter | solution.py:186
  428.9 0.7 copy-start.21
  526.3 10.4 %copy-start.11 = (bf16[4,16,4096]{2,1,0:T(8,128)(2,1)S(1)}, bf16[4,16,4096]{2,1,0:T(8,128)(2,1)}, u32[]{:S(2)}) copy-start(bf16[4,16,4096]{2,1,0:T(8,128)(2,1)} %param.21) | copy-start | bytes 1572868
  526.3 12.5 %copy-start.1 = (bf16[4096,160]{0,1:T(8,128)(2,1)S(1)}, bf16[4096,160]{0,1:T(8,128)(2,1)}, u32[]{:S(2)}) copy-start(bf16[4096,160]{0,1:T(8,128)(2,1)} %param.26) | copy-start | bytes 3932164
Sparse Core Ops, SparseCore 0:
  9.9 39.4 all-gather.6
  50.9 104.2 all-gather.8
  156.8 78.7 all-gather.12
  237.1 79.2 all-gather.10
  317.8 80.6 all-gather.14
  429.1 52.6 reduce-scatter.1
